TPU v7x, 512 devices: a whole 4x4x16 slice. The times are simulated.
512 devices in a mesh: req: 32 (over y, z_lo), head: 16 (over x, z_hi, core).
Axes of the slice: x: 4, y: 4, z: 16 (z_hi: 2, z_lo: 8; z = z_hi * 8 + z_lo), core: 2. Of those that a mesh axis runs over, the one named last changes fastest.
Arguments:
- hidden: bfloat16 [256, 2048], P('req', 'head'), may hold values from -6 to 6
- attn_gain: float32 [2048], replicated, may hold values from 0.1 to 1.9
- q_weight: bfloat16 [2048, 2048], P(None, 'head'), may hold values from -0.125 to 0.125
- gate_weight: bfloat16 [2048, 2048], P(None, 'head'), may hold values from -0.125 to 0.125
- key_value_weight: bfloat16 [2048, 2048], P(None, 'head'), may hold values from -0.125 to 0.125
- q_gain: float32 [128], replicated, may hold values from 0.5 to 1.5
- k_gain: float32 [128], replicated, may hold values from 0.5 to 2
- out_weight: bfloat16 [2048, 2048], P('head'), may hold values from -0.5 to 0.5
- prompt_key_cache: bfloat16 [32, 4096, 8, 128], P('req', 'head'), may hold values from -3.5 to 3.5
- prompt_value_cache: bfloat16 [32, 4096, 8, 128], P('req', 'head'), may hold values from -6 to 6
- tail_key_cache: bfloat16 [32, 4, 256, 8, 128], P('req', None, 'head'), may hold values from -3.5 to 3.5
- tail_value_cache: bfloat16 [32, 4, 256, 8, 128], P('req', None, 'head'), may hold values from -6 to 6
- mlp_gain: float32 [2048], replicated, may hold values from 0.1 to 1.9
- mlp_gate: bfloat16 [2048, 6144], P('req', 'head'), may hold values from -0.125 to 0.125
- mlp_up: bfloat16 [2048, 6144], P('req', 'head'), may hold values from -0.125 to 0.125
- mlp_down: bfloat16 [6144, 2048], P('head'), may hold values from -0.109375 to 0.109375
- final_gain: float32 [2048], P('head'), may hold values from 0.1 to 1.9
- score_weight: float32 [2048], P('head'), may hold values from -0.125 to 0.125
- prompt_lengths: int32 [32], replicated, may hold values from 1 to 4096, 65536 in all
- tail_lengths: int32 [32, 4], replicated, may hold values from 1 to 256, 512 in all within a row
- group_prompt: int32 [32], replicated, may hold values from 0 to 31, each once
Outputs:
- new_hidden: bfloat16 [256, 2048], P('req', 'head')
- score: float32 [256], P('req')
Inputs may be any that keep to these rules, and one draw needn't show every extreme that they name: `group_prompt`: every prompt is held by exactly one group. `prompt_lengths`: one prompt has exactly 4096 prefix tokens. `tail_lengths`: in every prompt one continuation has exactly 256 tail tokens.
All inputs are finite; a program needn't handle non-finite values.
Results may differ from a plain program's by a relative error of at most 0.023.
Values may be sent and summed in bfloat16 or wider, within the bound.
A program may use at most 64 MiB of HBM per device.

v0:
```python
import math
import jax
import jax.numpy as jnp
from jax import lax
from jax.sharding import PartitionSpec as P

EPS = 1e-06
THETA = 1000000.0


def rms_scale(value, gain):
    return value * lax.rsqrt(jnp.mean(value * value, axis=-1, keepdims=True) + EPS) * gain


def rotate(value, position):
    head_width = value.shape[-1]
    half_width = head_width // 2
    frequency = jnp.exp(
        -math.log(THETA) * 2.0 * jnp.arange(half_width, dtype=jnp.float32) / head_width
    )
    angles = position.astype(jnp.float32)[:, None] * frequency[None, :]
    cosine = jnp.cos(angles)[:, None, :]
    sine_part = jnp.sin(angles)[:, None, :]
    first_half = value[..., :half_width]
    second_half = value[..., half_width:]
    return jnp.concatenate(
        [
            first_half * cosine - second_half * sine_part,
            second_half * cosine + first_half * sine_part,
        ],
        axis=-1,
    )


def shards(
    hidden,
    attn_gain,
    q_weight,
    gate_weight,
    key_value_weight,
    q_gain,
    k_gain,
    out_weight,
    prompt_key_cache,
    prompt_value_cache,
    tail_key_cache,
    tail_value_cache,
    mlp_gain,
    mlp_gate,
    mlp_up,
    mlp_down,
    final_gain,
    score_weight,
    prompt_lengths,
    tail_lengths,
    group_prompt,
):
    head_count = lax.axis_size("head")
    group_count = lax.axis_size("req")
    group_id = lax.axis_index("req")
    head_place = lax.axis_index("head")
    count_of_rows = hidden.shape[0]
    model_width = attn_gain.shape[0]
    head_width = q_gain.shape[0]
    own_heads = q_weight.shape[1] // head_width
    all_heads = own_heads * head_count
    block_count = key_value_weight.shape[1] // head_width
    kv_heads = block_count * head_count // 2
    sharing_count = all_heads // kv_heads
    cont_count = tail_lengths.shape[1]
    new_count = count_of_rows // cont_count
    score_scale = 1.0 / math.sqrt(head_width)
    slot_ids = jnp.arange(group_count, dtype=jnp.int32)
    prompt_id = jnp.sum(jnp.where(slot_ids == group_id, group_prompt, 0))
    prompt_len = jnp.sum(jnp.where(slot_ids == prompt_id, prompt_lengths, 0))
    tail_row = jnp.sum(jnp.where((slot_ids == prompt_id)[:, None], tail_lengths, 0), axis=0)
    owner_group = jnp.sum(
        jnp.where(group_prompt[None, :] == slot_ids[:, None], slot_ids[None, :], 0), axis=1
    )
    position = (
        prompt_len + tail_row[:, None] + jnp.arange(new_count, dtype=jnp.int32)[None, :]
    ).reshape(count_of_rows)
    whole_rows = lax.all_gather(hidden, "head", axis=1, tiled=True)
    block_rows = whole_rows.astype(jnp.float32)
    normalized_hidden = rms_scale(block_rows, attn_gain).astype(jnp.bfloat16)
    gate_pre = jnp.dot(normalized_hidden, gate_weight, preferred_element_type=jnp.float32)
    query_rows = jnp.dot(normalized_hidden, q_weight, preferred_element_type=jnp.float32).reshape(
        count_of_rows, own_heads, head_width
    )
    query_rows = rotate(rms_scale(query_rows, q_gain), position).astype(jnp.bfloat16)
    projected_rows = jnp.dot(
        normalized_hidden, key_value_weight, preferred_element_type=jnp.float32
    ).reshape(count_of_rows, block_count, head_width)
    is_key = (head_place * block_count + jnp.arange(block_count, dtype=jnp.int32)) % 2 == 0
    keyed = rotate(rms_scale(projected_rows, k_gain), position)
    fresh = jnp.where(is_key[None, :, None], keyed, projected_rows).astype(jnp.bfloat16)
    all_queries, all_fresh = (
        lax.all_gather(
            query_rows.reshape(count_of_rows, own_heads * head_width), "head", axis=1, tiled=True
        ),
        lax.all_gather(
            fresh.reshape(count_of_rows, block_count * head_width), "head", axis=1, tiled=True
        ),
    )
    query_groups = all_queries.reshape(count_of_rows, kv_heads, sharing_count, head_width)
    local_keys = prompt_key_cache[0]
    local_values = prompt_value_cache[0]
    span_length = local_keys.shape[0]
    block_size = min(128, span_length)
    block_total = span_length // block_size
    span_start = head_place * span_length

    def prefix_block(block_id, sums):
        numer_acc, total_acc = sums
        key_block = lax.dynamic_slice_in_dim(local_keys, block_id * block_size, block_size, 0)
        value_block = lax.dynamic_slice_in_dim(local_values, block_id * block_size, block_size, 0)
        scores = (
            jnp.einsum(
                "rkgd,tkd->rkgt", query_groups, key_block, preferred_element_type=jnp.float32
            )
            * score_scale
        )
        slot_pos = span_start + block_id * block_size + jnp.arange(block_size, dtype=jnp.int32)
        attention_weights = jnp.where(
            slot_pos[None, None, None, :] < prompt_len, jnp.exp(scores), 0.0
        )
        numer_acc = numer_acc + jnp.einsum(
            "rkgt,tkd->rkgd",
            attention_weights.astype(jnp.bfloat16),
            value_block,
            preferred_element_type=jnp.float32,
        )
        return (numer_acc, total_acc + jnp.sum(attention_weights, axis=-1))

    start_sums = (
        jnp.zeros((count_of_rows, kv_heads, sharing_count, head_width), jnp.float32),
        jnp.zeros((count_of_rows, kv_heads, sharing_count), jnp.float32),
    )
    numerator, denominator = lax.fori_loop(0, block_total, prefix_block, start_sums)
    continuation_rows = query_groups.reshape(
        cont_count, new_count, kv_heads, sharing_count, head_width
    )
    tkeys = tail_key_cache[0]
    tail_value_rows = tail_value_cache[0]
    tail_span = tkeys.shape[1]
    scores = (
        jnp.einsum(
            "cjkgd,ctkd->cjkgt", continuation_rows, tkeys, preferred_element_type=jnp.float32
        )
        * score_scale
    )
    tail_pos = head_place * tail_span + jnp.arange(tail_span, dtype=jnp.int32)
    tail_live = tail_pos[None, :] < tail_row[:, None]
    attention_weights = jnp.where(tail_live[:, None, None, None, :], jnp.exp(scores), 0.0)
    numerator = numerator + jnp.einsum(
        "ihbyw,iwbs->ihbys",
        attention_weights.astype(jnp.bfloat16),
        tail_value_rows,
        preferred_element_type=jnp.float32,
    ).reshape(count_of_rows, kv_heads, sharing_count, head_width)
    denominator = denominator + jnp.sum(attention_weights, axis=-1).reshape(
        count_of_rows, kv_heads, sharing_count
    )
    numerator = numerator.reshape(count_of_rows, all_heads, head_width)
    denominator = denominator.reshape(count_of_rows, all_heads)
    numer_sum, total_sum = lax.psum((numerator, denominator), "head")
    numer_own = lax.dynamic_slice_in_dim(numer_sum, head_place * own_heads, own_heads, 1)
    total_own = lax.dynamic_slice_in_dim(total_sum, head_place * own_heads, own_heads, 1)
    fresh_all = all_fresh.reshape(count_of_rows, kv_heads, 2, head_width)
    own_kv = max(own_heads // sharing_count, 1)
    per_kv = own_heads // own_kv
    nearby = lax.dynamic_slice_in_dim(fresh_all, head_place * own_heads // sharing_count, own_kv, 1)
    own_queries = query_rows.reshape(cont_count, new_count, own_kv, per_kv, head_width)
    recent_key_rows = nearby[:, :, 0].reshape(cont_count, new_count, own_kv, head_width)
    recent_value_rows = nearby[:, :, 1].reshape(cont_count, new_count, own_kv, head_width)
    scores = (
        jnp.einsum(
            "cjkgd,cukd->cjkgu", own_queries, recent_key_rows, preferred_element_type=jnp.float32
        )
        * score_scale
    )
    causal = (
        jnp.arange(new_count, dtype=jnp.int32)[None, :]
        <= jnp.arange(new_count, dtype=jnp.int32)[:, None]
    )
    attention_weights = jnp.where(causal[None, :, None, None, :], jnp.exp(scores), 0.0)
    numer_own = numer_own + jnp.einsum(
        "bfmne,beml->bfmnl",
        attention_weights.astype(jnp.bfloat16),
        recent_value_rows,
        preferred_element_type=jnp.float32,
    ).reshape(count_of_rows, own_heads, head_width)
    total_own = total_own + jnp.sum(attention_weights, axis=-1).reshape(count_of_rows, own_heads)
    attention = (numer_own / total_own[..., None]).reshape(count_of_rows, own_heads * head_width)
    gated = (attention * jax.nn.sigmoid(gate_pre)).astype(jnp.bfloat16)
    mixed = lax.psum(jnp.dot(gated, out_weight, preferred_element_type=jnp.float32), "head")
    attended = (block_rows + mixed).astype(jnp.bfloat16)
    col_width = model_width // head_count
    wide_rows = attended.astype(jnp.float32)
    mlp_in = rms_scale(wide_rows, mlp_gain).astype(jnp.bfloat16)
    column_in = lax.all_to_all(mlp_in, "req", split_axis=1, concat_axis=0, tiled=True)
    gate_part = jnp.dot(column_in, mlp_gate, preferred_element_type=jnp.float32)
    up_part = jnp.dot(column_in, mlp_up, preferred_element_type=jnp.float32)
    gate_own, up_own = (
        lax.psum_scatter(gate_part, "req", scatter_dimension=0, tiled=True),
        lax.psum_scatter(up_part, "req", scatter_dimension=0, tiled=True),
    )
    act_rows = (jax.nn.silu(gate_own) * up_own).astype(jnp.bfloat16)
    down_part = jnp.dot(act_rows, mlp_down, preferred_element_type=jnp.float32)
    down_total = lax.psum(down_part, "head")
    added = lax.dynamic_slice_in_dim(down_total, head_place * col_width, col_width, 1)
    residual = lax.dynamic_slice_in_dim(wide_rows, head_place * col_width, col_width, 1)
    finished = (residual + added).astype(jnp.bfloat16)
    everyone = lax.all_gather(finished, "req", axis=0, tiled=True)
    my_owner = jnp.sum(jnp.where(slot_ids == group_id, owner_group, 0))
    new_hidden = lax.dynamic_slice_in_dim(everyone, my_owner * count_of_rows, count_of_rows, 0)
    final_rows = new_hidden.astype(jnp.float32)
    squares, product = lax.psum(
        (
            jnp.sum(final_rows * final_rows, axis=-1),
            jnp.sum(final_rows * final_gain * score_weight, axis=-1),
        ),
        "head",
    )
    score = product * lax.rsqrt(squares / model_width + EPS)
    return (new_hidden, score)


def solution(mesh):
    return jax.shard_map(
        shards,
        mesh=mesh,
        in_specs=(
            P("req", "head"),
            P(),
            P(None, "head"),
            P(None, "head"),
            P(None, "head"),
            P(),
            P(),
            P("head", None),
            P("req", "head", None, None),
            P("req", "head", None, None),
            P("req", None, "head", None, None),
            P("req", None, "head", None, None),
            P(),
            P("req", "head"),
            P("req", "head"),
            P("head", None),
            P("head"),
            P("head"),
            P(),
            P(),
            P(),
        ),
        out_specs=(P("req", "head"), P("req")),
        check_vma=False,
    )
```

profile of v0, /device:TPU:1, one launch (start us, length us, event | category | flops | bytes accessed | tf_op | source)
XLA Modules:
  0.0 1502.3 jit_solution(17086110039047880849)
XLA Ops:
  7.3 51.2 %all_gather.12 = bf16[8,2048]{1,0:T(8,128)(2,1)S(1)} all-gather(bf16[8,128]{1,0:T(8,128)(2,1)} %param.23), channel_id=1, replica_groups=mesh['req'=32,'head'=16] {'head'}, dimensions={1}, use_global_device_ids=true | all-gather | bytes 34816 | tf_op jit(solution)/shard_map/all_gather | solution.py:83
  58.4 0.1 fusion.23
  58.6 0.8 select_reduce_fusion
  59.3 1.3 fusion.70
  60.6 0.6 iota_compare_fusion.2
  61.3 2.0 select_reduce_fusion.2
  63.3 0.8 select_reduce_fusion.1
  64.1 0.7 broadcast_add_fusion
  65.0 1.4 multiply_reduce_fusion.2
  66.4 0.7 multiply_bitcast_fusion.1
  67.1 0.1 fusion.50
  67.3 33.8 %all_gather.13 = bf16[8,2048]{1,0:T(8,128)(2,1)S(1)} all-gather(bf16[8,128]{1,0:T(8,128)(2,1)S(1)} %pad_maximum_fusion), channel_id=1, replica_groups=mesh['req'=32,'head'=16] {'head'}, dimensions={1}, use_global_device_ids=true | all-gather | bytes 34816 | tf_op jit(solution)/shard_map/all_gather | solution.py:98
  101.1 1.4 copy_bitcast_fusion
  102.6 2.6 while.16
  102.6 0.8 add_compare_fusion.2
  103.3 0.3 fusion.110
  103.7 0.2 fusion.111
  103.9 0.7 add_compare_fusion.2
  104.6 0.3 fusion.110
  105.0 0.2 fusion.111
  105.3 0.3 fusion.85
  105.6 1.1 convolution_bitcast_fusion.1
  106.8 0.6 copy.83
  107.6 0.3 multiply_reduce_fusion.1
  108.0 0.1 fusion.54
  108.2 43.8 %all_gather.14 = bf16[8,2048]{1,0:T(8,128)(2,1)S(1)} all-gather(bf16[8,128]{1,0:T(8,128)(2,1)S(1)} %fusion.57), channel_id=1, replica_groups=mesh['req'=32,'head'=16] {'head'}, dimensions={1}, use_global_device_ids=true | all-gather | bytes 34816 | tf_op jit(solution)/shard_map/all_gather | solution.py:101
  152.1 0.2 fusion.14
  152.8 0.1 copy.87
  153.0 62.0 %psum.43 = f32[8,16]{0,1:T(8,128)S(1)} all-reduce(f32[8,16]{0,1:T(8,128)S(1)} %bitcast.127), channel_id=1, replica_groups=mesh['req'=32,'head'=16] {'head'}, use_global_device_ids=true, to_apply=%region_11.12 | all-reduce | flops 128 | bytes 1024 | tf_op jit(solution)/shard_map/psum | solution.py:166
  215.1 0.1 fusion.88
  215.2 132.7 %all-reduce.9.cloned.1.call-done = f32[8,16,128]{2,0,1:T(8,128)} async-done(((f32[8,16,128]{2,0,1:T(8,128)}), f32[8,16,128]{2,0,1:T(8,128)}) %all-reduce.9.cloned.1.call-update) | async-done | bytes 65552 | tf_op jit(solution)/shard_map/psum | solution.py:166
  347.9 1.7 fusion.20
  349.7 242.6 %all-reduce.11.cloned.1.call-done = f32[8,2048]{1,0:T(8,128)} async-done(((f32[8,2048]{1,0:T(8,128)}), f32[8,2048]{1,0:T(8,128)}) %all-reduce.11.cloned.1.call-update) | async-done | bytes 65552 | tf_op jit(solution)/shard_map/psum | solution.py:196
  592.3 1.0 multiply_reduce_fusion
  593.4 0.1 all_to_all.14
  593.6 0.1 reshape.325
  593.7 16.2 %all_to_all.19 = bf16[32,2,256]{2,1,0:T(2,128)(2,1)S(1)} all-to-all(bf16[32,2,256]{2,1,0:T(2,128)(2,1)S(1)} %reshape.325), channel_id=1, replica_groups=mesh['req'=32,'head'=16] {'req'}, dimensions={0} | all-to-all | bytes 65536 | tf_op jit(solution)/shard_map/all_to_all | solution.py:201
  610.1 0.9 fusion.27
  611.0 1.0 fusion.29
  612.0 1.3 dynamic-slice
  613.9 428.9 %all-reduce.15.cloned.1.call-done = (f32[256,384]{1,0:T(8,128)}, f32[256,384]{1,0:T(8,128)}) async-done(((f32[256,384]{1,0:T(8,128)}, f32[256,384]{1,0:T(8,128)}), (f32[256,384]{1,0:T(8,128)}, f32[256,384]{1,0:T(8,128)})) %all-reduce.15.cloned.1.call-update) | async-done | bytes 786448
  1042.8 1.7 fusion.35
  1045.2 263.3 %all-reduce.13.cloned.1.call-done = f32[8,2048]{1,0:T(8,128)} async-done(((f32[8,2048]{1,0:T(8,128)}), f32[8,2048]{1,0:T(8,128)}) %all-reduce.13.cloned.1.call-update) | async-done | bytes 65552 | tf_op jit(solution)/shard_map/psum | solution.py:210
  1308.5 0.7 add_convert_fusion
  1309.2 101.1 %all_gather.15 = bf16[256,128]{1,0:T(8,128)(2,1)S(1)} all-gather(bf16[8,128]{1,0:T(8,128)(2,1)S(1)} %add_convert_fusion), channel_id=1, replica_groups=mesh['req'=32,'head'=16] {'req'}, dimensions={0}, use_global_device_ids=true | all-gather | bytes 67584 | tf_op jit(solution)/shard_map/all_gather | solution.py:214
  1410.2 0.7 fusion.48
  1411.0 84.3 %all-reduce.3 = (f32[8]{0:T(128)S(1)}, f32[8]{0:T(128)S(1)}) all-reduce(f32[8]{0:T(128)S(1)} %get-tuple-element.172, f32[8]{0:T(128)S(1)} %get-tuple-element.171), channel_id=1, replica_groups=mesh['req'=32,'head'=16] {'head'}, use_global_device_ids=true, to_apply=%region_21.22 | all-reduce | flops 16 | bytes 128 | tf_op jit(solution)/shard_map/psum | solution.py:218
  1495.3 0.5 rsqrt_multiply_fusion
  (66 shorter events, 1.8 us)
Async XLA Ops:
  7.2 1035.7 %copy-start = (bf16[384,2048]{1,0:T(8,128)(2,1)S(1)}, bf16[384,2048]{1,0:T(8,128)(2,1)}, u32[]{:S(2)}) copy-start(bf16[384,2048]{1,0:T(8,128)(2,1)} %param.38) | copy-start | bytes 4718596
  7.2 340.7 %all-reduce.9.cloned.1.call-start = ((), (), s32[]{:S(2)}) async-start(), calls=%async_computation.1 | async-start | bytes 131072 | tf_op jit(solution)/shard_map/psum | solution.py:166
  102.5 2.8 copy-start.11
  102.5 5.0 copy-start.3
  102.5 5.0 copy-start.4
  105.2 2.8 copy-start.8
  105.2 242.7 %copy-start.1 = (bf16[128,2048]{1,0:T(8,128)(2,1)S(1)}, bf16[128,2048]{1,0:T(8,128)(2,1)}, u32[]{:S(2)}) copy-start(bf16[128,2048]{1,0:T(8,128)(2,1)} %param.30) | copy-start | bytes 1572868
  105.2 242.7 %copy-start.2 = (bf16[2048,128]{1,0:T(8,128)(2,1)S(1)}, bf16[2048,128]{1,0:T(8,128)(2,1)}, u32[]{:S(2)}) copy-start(bf16[2048,128]{1,0:T(8,128)(2,1)} %param.26) | copy-start | bytes 1572868
  105.6 487.7 %copy-start.7 = (f32[2048]{0:T(1024)S(1)}, f32[2048]{0:T(1024)}, u32[]{:S(2)}) copy-start(f32[2048]{0:T(1024)} %param.35) | copy-start | bytes 24580
  106.8 503.3 %copy-start.5 = (bf16[64,384]{1,0:T(8,128)(2,1)S(1)}, bf16[64,384]{1,0:T(8,128)(2,1)}, u32[]{:S(2)}) copy-start(bf16[64,384]{1,0:T(8,128)(2,1)} %param.37) | copy-start | bytes 147460
  107.4 484.9 %all-reduce.11.cloned.1.call-start = ((), (), s32[]{:S(2)}) async-start(), calls=%async_computation.2 | async-start | bytes 131072 | tf_op jit(solution)/shard_map/psum | solution.py:196
  107.6 503.4 %copy-start.6 = (bf16[64,384]{1,0:T(8,128)(2,1)S(1)}, bf16[64,384]{1,0:T(8,128)(2,1)}, u32[]{:S(2)}) copy-start(bf16[64,384]{1,0:T(8,128)(2,1)} %param.36) | copy-start | bytes 147460
  349.7 693.2 %all-reduce.15.cloned.1.call-start = ((), (), s32[]{:S(2)}) async-start(), calls=%async_computation.4 | async-start | bytes 1572864
  611.0 799.3 %copy-start.9 = (f32[128]{0:T(128)S(1)}, f32[128]{0:T(128)}, u32[]{:S(2)}) copy-start(f32[128]{0:T(128)} %param.40) | copy-start | bytes 1540
  611.0 799.3 %copy-start.10 = (f32[128]{0:T(128)S(1)}, f32[128]{0:T(128)}, u32[]{:S(2)}) copy-start(f32[128]{0:T(128)} %param.39) | copy-start | bytes 1540
  612.0 696.5 %all-reduce.13.cloned.1.call-start = ((), (), s32[]{:S(2)}) async-start(), calls=%async_computation.3 | async-start | bytes 131072 | tf_op jit(solution)/shard_map/psum | solution.py:210
Sparse Core Ops, SparseCore 0:
  107.6 240.3 all-reduce.8
  351.1 241.2 all-reduce.10
  612.1 430.6 all-reduce.14
  1045.9 262.5 all-reduce.12
where the time goes:
time: 1500 us
  waiting for transfers between devices  1070 us (71%)
  blocking collectives  392 us (26%)
  between operations  15.4 us (1%)
    unnamed x5, waiting for transfers between devices  429 us
    psum x1, waiting for transfers between devices, shards(): down_total = lax.psum(down_part, 'head')  263 us
    psum x1, waiting for transfers between devices, shards(): lax.psum(jnp.dot(gated, out_weight, preferred_element_type=jnp.float32),...  243 us
    psum x1, waiting for transfers between devices, shards(): numer_sum, total_sum = lax.psum((numerator, denominator), 'head')  133 us
    all_gather x1, blocking collectives, shards(): everyone = lax.all_gather(finished, 'req', axis=0, tiled=True)  101 us
    psum x1, blocking collectives, shards(): lax.psum((jnp.sum(final_rows * final_rows, axis=-1), jnp.sum(final_rows *...  84.3 us
    psum x1, blocking collectives, shards(): numer_sum, total_sum = lax.psum((numerator, denominator), 'head')  62 us
    all_gather x1, blocking collectives, shards(): whole_rows = lax.all_gather(hidden, 'head', axis=1, tiled=True)  51.2 us
  transfers between devices with their start and end apart: 4, of which 4 were waited for; matrix products, arithmetic and copies ran while one was open for 0% of the time, Pallas kernels for 0%

commit v1 on v0

--- a/solution.py
+++ b/solution.py
@@ -207,7 +207,7 @@
     )
     act_rows = (jax.nn.silu(gate_own) * up_own).astype(jnp.bfloat16)
     down_part = jnp.dot(act_rows, mlp_down, preferred_element_type=jnp.float32)
-    down_total = lax.psum(down_part, "head")
+    down_total = jnp.sum(lax.all_gather(down_part, "head"), axis=0)
     added = lax.dynamic_slice_in_dim(down_total, head_place * col_width, col_width, 1)
     residual = lax.dynamic_slice_in_dim(wide_rows, head_place * col_width, col_width, 1)
     finished = (residual + added).astype(jnp.bfloat16)

time: 1500 us -> 1330 us (0.89)
  waiting for transfers between devices: 1070 us -> 904 us
    psum x1 -> x0, waiting for transfers between devices: 263 us -> none  [shards(): down_total = lax.psum(down_part, 'head')]
    all_gather x0 -> x1, waiting for transfers between devices: none -> 99.8 us  [shards(): down_total = jnp.sum(lax.all_gather(down_part, 'head'), axis=0)]
where the time goes in v1:
time: 1330 us
  waiting for transfers between devices  904 us (68%)
  blocking collectives  383 us (29%)
  between operations  15.4 us (1%)
    unnamed x5, waiting for transfers between devices  429 us
    psum x1, waiting for transfers between devices, shards(): lax.psum(jnp.dot(gated, out_weight, preferred_element_type=jnp.float32),...  243 us
    psum x1, waiting for transfers between devices, shards(): numer_sum, total_sum = lax.psum((numerator, denominator), 'head')  133 us
    all_gather x1, blocking collectives, shards(): everyone = lax.all_gather(finished, 'req', axis=0, tiled=True)  100 us
    all_gather x1, waiting for transfers between devices, shards(): down_total = jnp.sum(lax.all_gather(down_part, 'head'), axis=0)  99.8 us
    psum x1, blocking collectives, shards(): lax.psum((jnp.sum(final_rows * final_rows, axis=-1), jnp.sum(final_rows *...  75.5 us
    psum x1, blocking collectives, shards(): numer_sum, total_sum = lax.psum((numerator, denominator), 'head')  62 us
    all_gather x1, blocking collectives, shards(): whole_rows = lax.all_gather(hidden, 'head', axis=1, tiled=True)  51.2 us
  transfers between devices with their start and end apart: 4, of which 4 were waited for; matrix products, arithmetic and copies ran while one was open for 0% of the time, Pallas kernels for 0%

profile of v1, /device:TPU:1, one launch (start us, length us, event | category | flops | bytes accessed | tf_op | source)
XLA Modules:
  0.0 1331.1 jit_solution(16153533904254058176)
XLA Ops:
  7.3 51.2 %all_gather.18 = bf16[8,2048]{1,0:T(8,128)(2,1)S(1)} all-gather(bf16[8,128]{1,0:T(8,128)(2,1)} %param.23), channel_id=1, replica_groups=mesh['req'=32,'head'=16] {'head'}, dimensions={1}, use_global_device_ids=true | all-gather | bytes 34816 | tf_op jit(solution)/shard_map/all_gather | solution.py:83
  58.4 0.1 fusion.23
  58.6 0.8 select_reduce_fusion
  59.3 1.3 fusion.70
  60.6 0.6 iota_compare_fusion.2
  61.3 2.0 select_reduce_fusion.2
  63.3 0.8 select_reduce_fusion.1
  64.1 0.7 broadcast_add_fusion
  65.0 1.4 multiply_reduce_fusion.2
  66.4 0.7 multiply_bitcast_fusion.1
  67.1 0.1 fusion.50
  67.3 33.8 %all_gather.19 = bf16[8,2048]{1,0:T(8,128)(2,1)S(1)} all-gather(bf16[8,128]{1,0:T(8,128)(2,1)S(1)} %pad_maximum_fusion), channel_id=1, replica_groups=mesh['req'=32,'head'=16] {'head'}, dimensions={1}, use_global_device_ids=true | all-gather | bytes 34816 | tf_op jit(solution)/shard_map/all_gather | solution.py:98
  101.1 1.4 copy_bitcast_fusion
  102.5 2.6 while.16
  102.6 0.7 add_compare_fusion.2
  103.3 0.3 fusion.110
  103.7 0.2 fusion.111
  103.9 0.7 add_compare_fusion.2
  104.6 0.3 fusion.110
  104.9 0.2 fusion.111
  105.3 1.3 fusion.85
  106.6 1.1 convolution_bitcast_fusion.1
  107.7 0.6 copy.83
  108.5 0.3 multiply_reduce_fusion.1
  109.0 0.1 fusion.54
  109.1 43.8 %all_gather.20 = bf16[8,2048]{1,0:T(8,128)(2,1)S(1)} all-gather(bf16[8,128]{1,0:T(8,128)(2,1)S(1)} %fusion.57), channel_id=1, replica_groups=mesh['req'=32,'head'=16] {'head'}, dimensions={1}, use_global_device_ids=true | all-gather | bytes 34816 | tf_op jit(solution)/shard_map/all_gather | solution.py:101
  153.0 0.2 fusion.14
  153.7 0.1 copy.87
  153.9 62.0 %psum.36 = f32[8,16]{0,1:T(8,128)S(1)} all-reduce(f32[8,16]{0,1:T(8,128)S(1)} %bitcast.129), channel_id=1, replica_groups=mesh['req'=32,'head'=16] {'head'}, use_global_device_ids=true, to_apply=%region_11.12 | all-reduce | flops 128 | bytes 1024 | tf_op jit(solution)/shard_map/psum | solution.py:166
  216.1 0.1 fusion.88
  216.2 132.7 %all-reduce.8.cloned.1.call-done = f32[8,16,128]{2,0,1:T(8,128)} async-done(((f32[8,16,128]{2,0,1:T(8,128)}), f32[8,16,128]{2,0,1:T(8,128)}) %all-reduce.8.cloned.1.call-update) | async-done | bytes 65552 | tf_op jit(solution)/shard_map/psum | solution.py:166
  348.9 1.7 fusion.20
  350.6 242.6 %all-reduce.10.cloned.1.call-done = f32[8,2048]{1,0:T(8,128)} async-done(((f32[8,2048]{1,0:T(8,128)}), f32[8,2048]{1,0:T(8,128)}) %all-reduce.10.cloned.1.call-update) | async-done | bytes 65552 | tf_op jit(solution)/shard_map/psum | solution.py:196
  593.2 1.0 multiply_reduce_fusion
  594.3 0.1 all_to_all.14
  594.5 0.1 reshape.326
  594.6 16.2 %all_to_all.19 = bf16[32,2,256]{2,1,0:T(2,128)(2,1)S(1)} all-to-all(bf16[32,2,256]{2,1,0:T(2,128)(2,1)S(1)} %reshape.326), channel_id=1, replica_groups=mesh['req'=32,'head'=16] {'req'}, dimensions={0} | all-to-all | bytes 65536 | tf_op jit(solution)/shard_map/all_to_all | solution.py:201
  611.0 0.9 fusion.27
  611.9 1.0 fusion.29
  613.0 1.3 dynamic-slice
  614.9 429.1 %all-reduce.12.cloned.1.call-done = (f32[256,384]{1,0:T(8,128)}, f32[256,384]{1,0:T(8,128)}) async-done(((f32[256,384]{1,0:T(8,128)}, f32[256,384]{1,0:T(8,128)}), (f32[256,384]{1,0:T(8,128)}, f32[256,384]{1,0:T(8,128)})) %all-reduce.12.cloned.1.call-update) | async-done | bytes 786448
  1044.0 1.7 fusion.35
  1046.3 99.8 %all-gather.3.cloned.1.call-done = f32[128,2048]{1,0:T(8,128)} async-done(((f32[8,2048]{1,0:T(8,128)}), f32[128,2048]{1,0:T(8,128)}) %all-gather.3.cloned.1.call-update) | async-done | bytes 1048592 | tf_op jit(solution)/shard_map/all_gather | solution.py:210
  1146.1 1.3 bitcast_reduce_fusion
  1147.4 100.4 %all_gather.23 = bf16[256,128]{1,0:T(8,128)(2,1)S(1)} all-gather(bf16[8,128]{1,0:T(8,128)(2,1)S(1)} %add_convert_fusion), channel_id=1, replica_groups=mesh['req'=32,'head'=16] {'req'}, dimensions={0}, use_global_device_ids=true | all-gather | bytes 67584 | tf_op jit(solution)/shard_map/all_gather | solution.py:214
  1247.8 0.7 fusion.48
  1248.6 75.5 %all-reduce.3 = (f32[8]{0:T(128)S(1)}, f32[8]{0:T(128)S(1)}) all-reduce(f32[8]{0:T(128)S(1)} %get-tuple-element.172, f32[8]{0:T(128)S(1)} %get-tuple-element.171), channel_id=1, replica_groups=mesh['req'=32,'head'=16] {'head'}, use_global_device_ids=true, to_apply=%region_21.22 | all-reduce | flops 16 | bytes 128 | tf_op jit(solution)/shard_map/psum | solution.py:218
  1324.0 0.5 rsqrt_multiply_fusion
  (65 shorter events, 1.8 us)
Async XLA Ops:
  7.2 1036.8 %copy-start = (bf16[384,2048]{1,0:T(8,128)(2,1)S(1)}, bf16[384,2048]{1,0:T(8,128)(2,1)}, u32[]{:S(2)}) copy-start(bf16[384,2048]{1,0:T(8,128)(2,1)} %param.38) | copy-start | bytes 4718596
  7.2 341.7 %all-reduce.8.cloned.1.call-start = ((), (), s32[]{:S(2)}) async-start(), calls=%async_computation.1 | async-start | bytes 131072 | tf_op jit(solution)/shard_map/psum | solution.py:166
  102.5 6.0 copy-start.3
  102.5 6.0 copy-start.4
  105.2 3.7 copy-start.8
  105.2 243.7 %copy-start.1 = (bf16[128,2048]{1,0:T(8,128)(2,1)S(1)}, bf16[128,2048]{1,0:T(8,128)(2,1)}, u32[]{:S(2)}) copy-start(bf16[128,2048]{1,0:T(8,128)(2,1)} %param.30) | copy-start | bytes 1572868
  105.2 243.7 %copy-start.2 = (bf16[2048,128]{1,0:T(8,128)(2,1)S(1)}, bf16[2048,128]{1,0:T(8,128)(2,1)}, u32[]{:S(2)}) copy-start(bf16[2048,128]{1,0:T(8,128)(2,1)} %param.26) | copy-start | bytes 1572868
  106.6 487.7 %copy-start.7 = (f32[2048]{0:T(1024)S(1)}, f32[2048]{0:T(1024)}, u32[]{:S(2)}) copy-start(f32[2048]{0:T(1024)} %param.35) | copy-start | bytes 24580
  107.7 503.3 %copy-start.5 = (bf16[64,384]{1,0:T(8,128)(2,1)S(1)}, bf16[64,384]{1,0:T(8,128)(2,1)}, u32[]{:S(2)}) copy-start(bf16[64,384]{1,0:T(8,128)(2,1)} %param.37) | copy-start | bytes 147460
  108.4 484.9 %all-reduce.10.cloned.1.call-start = ((), (), s32[]{:S(2)}) async-start(), calls=%async_computation.2 | async-start | bytes 131072 | tf_op jit(solution)/shard_map/psum | solution.py:196
  108.5 503.4 %copy-start.6 = (bf16[64,384]{1,0:T(8,128)(2,1)S(1)}, bf16[64,384]{1,0:T(8,128)(2,1)}, u32[]{:S(2)}) copy-start(bf16[64,384]{1,0:T(8,128)(2,1)} %param.36) | copy-start | bytes 147460
  350.6 693.4 %all-reduce.12.cloned.1.call-start = ((), (), s32[]{:S(2)}) async-start(), calls=%async_computation.4 | async-start | bytes 1572864
  612.9 635.0 %copy-start.9 = (f32[128]{0:T(128)S(1)}, f32[128]{0:T(128)}, u32[]{:S(2)}) copy-start(f32[128]{0:T(128)} %param.40) | copy-start | bytes 1540
  612.9 635.0 %copy-start.10 = (f32[128]{0:T(128)S(1)}, f32[128]{0:T(128)}, u32[]{:S(2)}) copy-start(f32[128]{0:T(128)} %param.39) | copy-start | bytes 1540
  612.9 533.2 %all-gather.3.cloned.1.call-start = ((), (), s32[]{:S(2)}) async-start(), calls=%async_computation.3 | async-start | bytes 1114112 | tf_op jit(solution)/shard_map/all_gather | solution.py:210
Sparse Core Ops, SparseCore 0:
  108.5 240.3 all-reduce.7
  352.0 241.1 all-reduce.9
  613.0 430.9 all-reduce.11
  1047.6 98.4 all-gather.2
